TPU v7x, 128 devices: a whole 4x4x4 slice. The times are simulated.
128 devices in a mesh: section: 16 (over x_hi, y, core), dp: 8 (over x_lo, z).
Axes of the slice: x: 4 (x_hi: 2, x_lo: 2; x = x_hi * 2 + x_lo), y: 4, z: 4, core: 2. Of those that a mesh axis runs over, the one named last changes fastest.
Arguments:
- master_weights: float32 [16, 8192, 512], P('section', 'dp'), may hold values from -0.0625 to 0.0625
- first_moment: float32 [16, 8192, 512], P('section', 'dp'), may hold values from -2 to 2
- second_moment: float32 [16, 8192, 512], P('section', 'dp'), may hold values from 0.05 to 2
- gradient_shard: float32 [16, 8192, 512], P('section', 'dp'), may hold values from -6 to 6
- hidden_states: bfloat16 [16, 2, 1024, 8192], P('section', None, 'dp'), may hold values from -6 to 6
Outputs:
- new_master: float32 [16, 8192, 512], P('section', 'dp')
- new_first: float32 [16, 8192, 512], P('section', 'dp')
- new_second: float32 [16, 8192, 512], P('section', 'dp')
- hidden_out: bfloat16 [16, 2, 1024, 8192], P('section', None, 'dp')
All inputs are finite; a program needn't handle non-finite values.
Results may differ from a plain program's by a relative error of at most 0.008.
Values may be sent and summed in bfloat16 or wider, within the bound.
No kernel may reach another device: no remote copies, remote signals or barrier semaphores. Data moves between devices by JAX's collectives and lax.ppermute only.
A program may use at most 192 MiB of HBM per device.

v0:
```python
import jax
import jax.numpy as jnp
from jax import lax
from jax.sharding import PartitionSpec as P

ROUNDS = 4
ADAM_STEP = 1000


beta_one = 0.9
beta_two = 0.95
learn_rate = 0.0003
decay_rate = 0.1
adam_eps = 1e-08
norm_eps = 1e-05


def from_behind(value, axis, steps):
    count = lax.axis_size(axis)
    pairs = [(source, (source + steps) % count) for source in range(count)]
    return lax.ppermute(value, axis, pairs)


def adamw_update(master, moment, second, gradient):
    moment_new = beta_one * moment + (1.0 - beta_one) * gradient
    second_new = beta_two * second + (1.0 - beta_two) * gradient * gradient
    corr_one = 1.0 - beta_one**ADAM_STEP
    corr_two = 1.0 - beta_two**ADAM_STEP
    step_size = moment_new / corr_one / (jnp.sqrt(second_new / corr_two) + adam_eps)
    master_new = master - learn_rate * (step_size + decay_rate * master)
    return (master_new, moment_new, second_new)


def normalize(block):
    flat = block.astype(jnp.float32)
    return (flat * lax.rsqrt(jnp.mean(flat * flat, axis=-1, keepdims=True) + norm_eps)).astype(
        jnp.bfloat16
    )


def project(normed, weight):
    return jnp.dot(normed, weight, preferred_element_type=jnp.float32).astype(jnp.bfloat16)


def expand(block, projected, weight):
    update = lax.dot_general(
        projected, weight, (((1,), (1,)), ((), ())), preferred_element_type=jnp.float32
    )
    return (block.astype(jnp.float32) + update).astype(jnp.bfloat16)


def per_device(master_weights, first_moment, second_moment, gradient_shard, hidden_states):
    new_master, new_first, new_second = adamw_update(
        master_weights, first_moment, second_moment, gradient_shard
    )
    local_rows = new_master[0].astype(jnp.bfloat16)
    count = hidden_states.shape[1]
    rows = hidden_states.shape[2]
    current = hidden_states[0]
    first_proj = None
    full_weight = lax.all_gather(local_rows, "dp", axis=0, tiled=True)
    for step in range(ROUNDS):
        results = []
        for index in range(count):
            block = current[index]
            projected = project(normalize(block), full_weight)
            result = expand(block, projected, full_weight)
            results.append(result)
        current = jnp.stack(results)
        current = from_behind(current, "section", 1)
    return (new_master, new_first, new_second, current[None])


def solution(mesh):
    placed = (
        P("section", "dp", None),
        P("section", "dp", None),
        P("section", "dp", None),
        P("section", "dp", None),
        P("section", None, "dp", None),
    )
    return jax.shard_map(
        per_device,
        mesh=mesh,
        in_specs=placed,
        out_specs=(
            P("section", "dp", None),
            P("section", "dp", None),
            P("section", "dp", None),
            P("section", None, "dp", None),
        ),
        check_vma=False,
    )
```

profile of v0, /device:TPU:0, one launch (start us, length us, event | category | flops | bytes accessed | tf_op | source)
XLA Modules:
  0.0 435.9 jit_solution(11725104187381646436)
XLA Ops:
  7.2 0.0 all-gather.3.cloned.1.call-start
  7.2 7.5 %fusion.149 = (bf16[1,1024,512]{2,1,0:T(8,128)(2,1)}, f32[1,1024,512]{2,1,0:T(8,128)}, f32[1,1024,512]{2,1,0:T(8,128)}, f32[1,1024,512]{2,1,0:T(8,128)}) fusion(f32[1,1024,512]{2,1,0:T(8,128)} %param.5, f32[1,1024,512]{2,1,0:T(8,128)} %param.8, f32[1,1024,512]{2,1,0:T(8,128)} %param.7, f32[1,1024,512]{2,1,0:T(8,128)} %param.6), kind=kLoop, calls=%fused_computation.122 | loop fusion | flops 7340032 | bytes 15728640 | tf_op jit(solution)/shard_map/convert_element_type | solution.py:56
  14.7 0.0 all-gather.3.cloned.1.call-update
  14.7 3.1 fusion.40
  17.9 91.6 %all-gather.3.cloned.1.call-done = bf16[1,8192,512]{2,1,0:T(8,128)(2,1)} async-done(((bf16[1,1024,512]{2,1,0:T(8,128)(2,1)}), bf16[1,8192,512]{2,1,0:T(8,128)(2,1)}) %all-gather.3.cloned.1.call-update) | async-done | bytes 8388624 | tf_op jit(solution)/shard_map/all_gather | solution.py:61
  109.4 11.1 %fusion.14 = bf16[1,128,8192]{2,1,0:T(8,128)(2,1)S(1)} fusion(bf16[1,8192,512]{2,1,0:T(8,128)(2,1)} %all-gather.3.cloned.1.call-done, bf16[1,2,128,8192]{3,2,1,0:T(8,128)(2,1)} %param.9, f32[128]{0:T(128)S(1)} %get-tuple-element.16), kind=kOutput, calls=%fused_computation.22 | convolution fusion | flops 2153840640 | bytes 23069184 | tf_op jit(solution)/shard_map/dot_general | solution.py:46
  120.5 12.3 %fusion.15 = bf16[1,128,8192]{2,1,0:T(8,128)(2,1)} fusion(bf16[1,8192,512]{2,1,0:T(8,128)(2,1)} %all-gather.3.cloned.1.call-done, bf16[1,2,128,8192]{3,2,1,0:T(8,128)(2,1)} %param.9, f32[128]{0:T(128)S(1)} %get-tuple-element.17), kind=kOutput, calls=%fused_computation.23 | convolution fusion | flops 2153840640 | bytes 23069184 | tf_op jit(solution)/shard_map/dot_general | solution.py:46
  132.8 2.0 pad_maximum_fusion
  134.8 0.3 collective-permute-start
  135.1 51.5 %collective-permute-done = bf16[2,128,8192]{2,1,0:T(8,128)(2,1)S(1)} collective-permute-done((bf16[2,128,8192]{2,1,0:T(8,128)(2,1)S(1)}, bf16[2,128,8192]{2,1,0:T(8,128)(2,1)S(1)}, u32[]{:S(2)}, u32[]{:S(2)}) %collective-permute-start) | collective-permute-done | bytes 4194336 | tf_op jit(solution)/shard_map/ppermute | solution.py:21
  186.6 0.0 copy-start.1
  186.6 2.0 copy-done.1
  188.6 0.9 fusion.44
  189.5 11.1 %fusion.12 = bf16[1,128,8192]{2,1,0:T(8,128)(2,1)S(1)} fusion(bf16[1,8192,512]{2,1,0:T(8,128)(2,1)} %all-gather.3.cloned.1.call-done, bf16[2,128,8192]{2,1,0:T(8,128)(2,1)} %copy-done.1, f32[128]{0:T(128)S(1)} %add_rsqrt_fusion.4), kind=kOutput, calls=%fused_computation.20 | convolution fusion | flops 2153840640 | bytes 23069184 | tf_op jit(solution)/shard_map/dot_general | solution.py:46
  200.6 12.4 %fusion.13 = bf16[1,128,8192]{2,1,0:T(8,128)(2,1)} fusion(bf16[1,8192,512]{2,1,0:T(8,128)(2,1)} %all-gather.3.cloned.1.call-done, bf16[2,128,8192]{2,1,0:T(8,128)(2,1)} %copy-done.1, f32[128]{0:T(128)S(1)} %add_rsqrt_fusion.5), kind=kOutput, calls=%fused_computation.21 | convolution fusion | flops 2153840640 | bytes 23069184 | tf_op jit(solution)/shard_map/dot_general | solution.py:46
  213.0 2.0 pad_maximum_fusion.1
  215.0 0.3 collective-permute-start.1
  215.3 51.5 %collective-permute-done.1 = bf16[2,128,8192]{2,1,0:T(8,128)(2,1)S(1)} collective-permute-done((bf16[2,128,8192]{2,1,0:T(8,128)(2,1)S(1)}, bf16[2,128,8192]{2,1,0:T(8,128)(2,1)S(1)}, u32[]{:S(2)}, u32[]{:S(2)}) %collective-permute-start.1) | collective-permute-done | bytes 4194336 | tf_op jit(solution)/shard_map/ppermute | solution.py:21
  266.8 0.0 copy-start.2
  266.8 2.0 copy-done.2
  268.8 0.9 fusion.48
  269.8 11.1 %fusion.10 = bf16[1,128,8192]{2,1,0:T(8,128)(2,1)S(1)} fusion(bf16[1,8192,512]{2,1,0:T(8,128)(2,1)} %all-gather.3.cloned.1.call-done, bf16[2,128,8192]{2,1,0:T(8,128)(2,1)} %copy-done.2, f32[128]{0:T(128)S(1)} %add_rsqrt_fusion.2), kind=kOutput, calls=%fused_computation.18 | convolution fusion | flops 2153840640 | bytes 23069184 | tf_op jit(solution)/shard_map/dot_general | solution.py:46
  280.8 12.4 %fusion.11 = bf16[1,128,8192]{2,1,0:T(8,128)(2,1)} fusion(bf16[1,8192,512]{2,1,0:T(8,128)(2,1)} %all-gather.3.cloned.1.call-done, bf16[2,128,8192]{2,1,0:T(8,128)(2,1)} %copy-done.2, f32[128]{0:T(128)S(1)} %add_rsqrt_fusion.3), kind=kOutput, calls=%fused_computation.19 | convolution fusion | flops 2153840640 | bytes 23069184 | tf_op jit(solution)/shard_map/dot_general | solution.py:46
  293.2 2.0 pad_maximum_fusion.2
  295.2 0.3 collective-permute-start.2
  295.5 51.5 %collective-permute-done.2 = bf16[2,128,8192]{2,1,0:T(8,128)(2,1)S(1)} collective-permute-done((bf16[2,128,8192]{2,1,0:T(8,128)(2,1)S(1)}, bf16[2,128,8192]{2,1,0:T(8,128)(2,1)S(1)}, u32[]{:S(2)}, u32[]{:S(2)}) %collective-permute-start.2) | collective-permute-done | bytes 4194336 | tf_op jit(solution)/shard_map/ppermute | solution.py:21
  347.1 0.0 copy-start
  347.1 2.0 copy-done
  349.1 0.9 fusion.52
  350.0 11.1 %fusion.8 = bf16[1,128,8192]{2,1,0:T(8,128)(2,1)S(1)} fusion(bf16[1,8192,512]{2,1,0:T(8,128)(2,1)} %all-gather.3.cloned.1.call-done, bf16[2,128,8192]{2,1,0:T(8,128)(2,1)} %copy-done, f32[128]{0:T(128)S(1)} %add_rsqrt_fusion), kind=kOutput, calls=%fused_computation.16 | convolution fusion | flops 2153840640 | bytes 23069184 | tf_op jit(solution)/shard_map/dot_general | solution.py:46
  361.1 12.4 %fusion.9 = bf16[1,128,8192]{2,1,0:T(8,128)(2,1)} fusion(bf16[1,8192,512]{2,1,0:T(8,128)(2,1)} %all-gather.3.cloned.1.call-done, bf16[2,128,8192]{2,1,0:T(8,128)(2,1)} %copy-done, f32[128]{0:T(128)S(1)} %add_rsqrt_fusion.1), kind=kOutput, calls=%fused_computation.17 | convolution fusion | flops 2153840640 | bytes 23069184 | tf_op jit(solution)/shard_map/dot_general | solution.py:46
  373.5 2.0 pad_maximum_fusion.3
  375.5 0.1 collective-permute-start.3
  375.5 51.5 %collective-permute-done.3 = bf16[2,128,8192]{2,1,0:T(8,128)(2,1)S(1)} collective-permute-done((bf16[2,128,8192]{2,1,0:T(8,128)(2,1)S(1)}, bf16[2,128,8192]{2,1,0:T(8,128)(2,1)S(1)}, u32[]{:S(2)}, u32[]{:S(2)}) %collective-permute-start.3) | collective-permute-done | bytes 4194336 | tf_op jit(solution)/shard_map/ppermute | solution.py:21
  427.1 2.0 copy.10
  (7 shorter events, 0.0 us)
Async XLA Ops:
  7.2 102.3 %all-gather.3.cloned.1.call-start = ((), (), s32[]{:S(2)}) async-start(), calls=%async_computation | async-start | bytes 9437184 | tf_op jit(solution)/shard_map/all_gather | solution.py:61
  134.8 51.8 %collective-permute-start = (bf16[2,128,8192]{2,1,0:T(8,128)(2,1)S(1)}, bf16[2,128,8192]{2,1,0:T(8,128)(2,1)S(1)}, u32[]{:S(2)}, u32[]{:S(2)}) collective-permute-start(bf16[2,128,8192]{2,1,0:T(8,128)(2,1)S(1)} %pad_maximum_fusion), channel_id=1, source_target_pairs={{0,8},{8,16},{16,24},{24,32},{32,40},{40,48},{48,56},{56,64},{64,7... | collective-permute-start | bytes 12582920 | tf_op jit(solution)/shard_map/ppermute | solution.py:21
  186.6 2.0 copy-start.1
  215.0 51.8 %collective-permute-start.1 = (bf16[2,128,8192]{2,1,0:T(8,128)(2,1)S(1)}, bf16[2,128,8192]{2,1,0:T(8,128)(2,1)S(1)}, u32[]{:S(2)}, u32[]{:S(2)}) collective-permute-start(bf16[2,128,8192]{2,1,0:T(8,128)(2,1)S(1)} %pad_maximum_fusion.1), channel_id=1, source_target_pairs={{0,8},{8,16},{16,24},{24,32},{32,40},{40,48},{48,56},{56,64},{64,7... | collective-permute-start | bytes 12582920 | tf_op jit(solution)/shard_map/ppermute | solution.py:21
  266.8 2.0 copy-start.2
  295.2 51.9 %collective-permute-start.2 = (bf16[2,128,8192]{2,1,0:T(8,128)(2,1)S(1)}, bf16[2,128,8192]{2,1,0:T(8,128)(2,1)S(1)}, u32[]{:S(2)}, u32[]{:S(2)}) collective-permute-start(bf16[2,128,8192]{2,1,0:T(8,128)(2,1)S(1)} %pad_maximum_fusion.2), channel_id=1, source_target_pairs={{0,8},{8,16},{16,24},{24,32},{32,40},{40,48},{48,56},{56,64},{64,7... | collective-permute-start | bytes 12582920 | tf_op jit(solution)/shard_map/ppermute | solution.py:21
  347.1 2.0 copy-start
  375.5 51.6 %collective-permute-start.3 = (bf16[2,128,8192]{2,1,0:T(8,128)(2,1)S(1)}, bf16[2,128,8192]{2,1,0:T(8,128)(2,1)S(1)}, u32[]{:S(2)}, u32[]{:S(2)}) collective-permute-start(bf16[2,128,8192]{2,1,0:T(8,128)(2,1)S(1)} %pad_maximum_fusion.3), channel_id=1, source_target_pairs={{0,8},{8,16},{16,24},{24,32},{32,40},{40,48},{48,56},{56,64},{64,7... | collective-permute-start | bytes 12582920 | tf_op jit(solution)/shard_map/ppermute | solution.py:21
Sparse Core Ops, SparseCore 0:
  14.8 94.5 all-gather.2
where the time goes:
time: 436 us
  waiting for transfers between devices  298 us (68%)
  matrix products  93.7 us (21%)
  other arithmetic  21.3 us (5%)
  between operations  14.1 us (3%)
  local copies, waits for them, and re-layouts  8.05 us (2%)
    ppermute x4, waiting for transfers between devices, from_behind(): return lax.ppermute(value, axis, pairs)  206 us
    dot_general x8, matrix products, expand(): lax.dot_general(projected, weight, (((1,), (1,)), ((), ())), preferred_el...  93.7 us
    all_gather x1, waiting for transfers between devices, per_device(): full_weight = lax.all_gather(local_rows, 'dp', axis=0, tiled=True)  91.6 us
  transfers between devices with their start and end apart: 5, of which 5 were waited for; matrix products, arithmetic and copies ran while one was open for 1% of the time, Pallas kernels for 0%

commit v1 on v0

v1 whole, which is shorter than its diff:
```python
import functools

import jax
import jax.numpy as jnp
from jax import lax
from jax.experimental import pallas as pl
from jax.experimental.pallas import tpu as pltpu
from jax.sharding import PartitionSpec as P

ADAM_STEP = 1000

beta_one = 0.9
beta_two = 0.95
learn_rate = 0.0003
decay_rate = 0.1
adam_eps = 1e-08
norm_eps = 1e-05

AXES = ("section", "dp")
D = 8192
KVW = 512
ROWS = 256
SUB = 512
HALF = D // 2
LANES = 128
VMEM = 56 * 1024 * 1024


def place(linear):
    section, dp = divmod(linear, 8)
    return section // 2, section % 2, dp // 4, dp % 4


def linear_of(chip, core, xlo, z):
    return ((chip % 8) * 2 + core) * 8 + (xlo % 2) * 4 + z % 4


def shift(value, move):
    pairs = [(source, linear_of(*move(*place(source)))) for source in range(128)]
    return lax.ppermute(value, AXES, pairs)


def to_core(value):
    return shift(value, lambda chip, core, xlo, z: (chip, 1 - core, xlo, z))


def to_pair(value):
    return shift(value, lambda chip, core, xlo, z: (chip, core, xlo + 1, z))


def to_ring(value):
    return shift(value, lambda chip, core, xlo, z: (chip, core, xlo, z + 1 - 2 * core))


def to_chip(value, steps):
    return shift(value, lambda chip, core, xlo, z: (chip + steps, core, xlo, z))


def adamw_update(master, moment, second, gradient):
    moment_new = beta_one * moment + (1.0 - beta_one) * gradient
    second_new = beta_two * second + (1.0 - beta_two) * gradient * gradient
    corr_one = 1.0 - beta_one**ADAM_STEP
    corr_two = 1.0 - beta_two**ADAM_STEP
    step_size = moment_new / corr_one / (jnp.sqrt(second_new / corr_two) + adam_eps)
    master_new = master - learn_rate * (step_size + decay_rate * master)
    return (master_new, moment_new, second_new)


def split_kernel(core_ref, whole_ref, keep_ref, give_ref):
    first = whole_ref[:, :SUB]
    last = whole_ref[:, SUB:]
    upper = core_ref[0] == 1
    keep_ref[...] = jnp.where(upper, last, first)
    give_ref[...] = jnp.where(upper, first, last)


def split_halves(core, whole):
    spec = pl.BlockSpec((ROWS, SUB), lambda i, core: (0, i))
    return pl.pallas_call(
        split_kernel,
        grid_spec=pltpu.PrefetchScalarGridSpec(
            num_scalar_prefetch=1,
            grid=(8,),
            in_specs=[pl.BlockSpec((ROWS, 2 * SUB), lambda i, core: (0, i))],
            out_specs=[spec, spec],
        ),
        out_shape=[jax.ShapeDtypeStruct((ROWS, HALF), jnp.bfloat16)] * 2,
        cost_estimate=pl.CostEstimate(flops=0, bytes_accessed=8 << 20, transcendentals=0),
        name="split_halves",
    )(core, whole)


def merge_kernel(core_ref, keep_ref, got_ref, whole_ref):
    upper = core_ref[0] == 1
    keep = keep_ref[...]
    got = got_ref[...]
    whole_ref[:, :SUB] = jnp.where(upper, got, keep)
    whole_ref[:, SUB:] = jnp.where(upper, keep, got)


def merge_halves(core, keep, got):
    spec = pl.BlockSpec((ROWS, SUB), lambda i, core: (0, i))
    return pl.pallas_call(
        merge_kernel,
        grid_spec=pltpu.PrefetchScalarGridSpec(
            num_scalar_prefetch=1,
            grid=(8,),
            in_specs=[spec, spec],
            out_specs=pl.BlockSpec((ROWS, 2 * SUB), lambda i, core: (0, i)),
        ),
        out_shape=jax.ShapeDtypeStruct((ROWS, D), jnp.bfloat16),
        cost_estimate=pl.CostEstimate(flops=0, bytes_accessed=8 << 20, transcendentals=0),
        name="merge_halves",
    )(core, keep, got)


def columns_of(place_ref, step, xlo):
    return pl.ds(pl.multiple_of(place_ref[step * 2 + xlo], SUB), SUB)


def project_into(place_ref, hidden, weights, out_ref):
    rows = out_ref.shape[0]
    total = jnp.zeros((rows, KVW), jnp.float32)
    squares = jnp.zeros((rows, 1), jnp.float32)
    for step in range(4):
        for xlo in range(2):
            part = hidden[:, columns_of(place_ref, step, xlo)]
            total += jnp.dot(
                part,
                weights[step][xlo * SUB : (xlo + 1) * SUB, :],
                preferred_element_type=jnp.float32,
            )
            flat = part.astype(jnp.float32)
            squares += jnp.sum(flat * flat, axis=1, keepdims=True)
    out_ref[:, :KVW] = total
    out_ref[:, KVW:] = jnp.broadcast_to(squares, (rows, LANES))


def expand_into(place_ref, hidden, mine, theirs, weights, out_ref):
    summed = mine[...] + theirs[...]
    scale = lax.rsqrt(summed[:, KVW : KVW + 1] * (1.0 / D) + norm_eps)
    projected = (summed[:, :KVW] * scale).astype(jnp.bfloat16)
    for step in range(4):
        for xlo in range(2):
            columns = columns_of(place_ref, step, xlo)
            update = lax.dot_general(
                projected,
                weights[step][xlo * SUB : (xlo + 1) * SUB, :],
                (((1,), (1,)), ((), ())),
                preferred_element_type=jnp.float32,
            )
            out_ref[:, columns] = (hidden[:, columns].astype(jnp.float32) + update).astype(
                jnp.bfloat16
            )


def project_kernel(place_ref, hidden, w0, w1, w2, w3, out_ref):
    project_into(place_ref, hidden, (w0, w1, w2, w3), out_ref)


def expand_kernel(place_ref, hidden, mine, theirs, w0, w1, w2, w3, out_ref):
    expand_into(place_ref, hidden, mine, theirs, (w0, w1, w2, w3), out_ref)


def whole_call(kernel, out_shape, place, operands, flops, name):
    moved = sum(a.size * a.dtype.itemsize for a in operands)
    moved += sum(a.size * a.dtype.itemsize for a in jax.tree.leaves(out_shape))
    return pl.pallas_call(
        kernel,
        in_specs=[pl.BlockSpec(memory_space=pltpu.SMEM)]
        + [pl.BlockSpec(memory_space=pltpu.VMEM)] * len(operands),
        out_specs=jax.tree.map(lambda a: pl.BlockSpec(memory_space=pltpu.VMEM), out_shape),
        out_shape=out_shape,
        compiler_params=pltpu.CompilerParams(vmem_limit_bytes=VMEM),
        cost_estimate=pl.CostEstimate(flops=flops, bytes_accessed=moved, transcendentals=0),
        name=name,
    )(place, *operands)


def project(place, hidden, weights):
    rows = hidden.shape[0]
    return whole_call(
        project_kernel,
        jax.ShapeDtypeStruct((rows, KVW + LANES), jnp.float32),
        place,
        (hidden, *weights),
        2 * rows * HALF * KVW,
        "project",
    )


def expand(place, hidden, mine, theirs, weights):
    rows = hidden.shape[0]
    return whole_call(
        expand_kernel,
        jax.ShapeDtypeStruct((rows, HALF), jnp.bfloat16),
        place,
        (hidden, mine, theirs, *weights),
        2 * rows * HALF * KVW,
        "expand",
    )


def apply_layer(place, hidden, weights):
    mine = project(place, hidden, weights)
    return expand(place, hidden, mine, to_core(mine), weights)


def gather_pieces(own, xlo):
    other = to_pair(own)
    lower = xlo == 0
    piece = jnp.concatenate([jnp.where(lower, own, other), jnp.where(lower, other, own)], axis=0)
    pieces = [piece]
    for _ in range(3):
        pieces.append(to_ring(pieces[-1]))
    return pieces


def per_device(master_weights, first_moment, second_moment, gradient_shard, hidden_states):
    core = lax.rem(lax.axis_index("section"), 2)
    xlo = lax.div(lax.axis_index("dp"), 4)
    z = lax.rem(lax.axis_index("dp"), 4)
    upper = core == 1
    core_word = jnp.reshape(core, (1,)).astype(jnp.int32)
    step = jnp.arange(4, dtype=jnp.int32)
    owner = lax.rem(z + jnp.where(upper, step, 4 - step), 4)
    table = jnp.stack([owner * SUB, (owner + 4) * SUB], axis=1).reshape(8).astype(jnp.int32)

    block = hidden_states.reshape(ROWS, D)
    keep, give = split_halves(core_word, block)
    got = to_core(give)
    even = jnp.where(upper, got, keep)
    odd = jnp.where(upper, keep, got)
    odd = to_chip(odd, 2)

    new_master, new_first, new_second = adamw_update(
        master_weights, first_moment, second_moment, gradient_shard
    )
    rows = new_master[0].astype(jnp.bfloat16)
    mine = lax.dynamic_slice_in_dim(rows, core * SUB, SUB, 0)
    theirs = lax.dynamic_slice_in_dim(rows, (1 - core) * SUB, SUB, 0)
    other = to_core(theirs)
    even_rows = jnp.where(upper, other, mine)
    odd_rows = jnp.where(upper, mine, other)

    home = gather_pieces(even_rows, xlo)
    far = to_chip(odd_rows, 2)
    near = to_chip(jnp.concatenate([even_rows, odd_rows], axis=0), 1)
    first = gather_pieces(far, xlo)
    second = gather_pieces(near[:SUB], xlo)
    third = gather_pieces(near[SUB:], xlo)

    even = to_chip(apply_layer(table, even, home), 2)
    both = jnp.concatenate([even, odd], axis=0)
    both = apply_layer(table, both, first)
    both = apply_layer(table, both, second)
    both = apply_layer(table, both, third)
    even = both[:ROWS]
    odd = apply_layer(table, both[ROWS:], home)
    keep = jnp.where(upper, odd, even)
    give = jnp.where(upper, even, odd)
    out = merge_halves(core_word, keep, to_core(give))
    return (new_master, new_first, new_second, out.reshape(hidden_states.shape))


def solution(mesh):
    placed = (
        P("section", "dp", None),
        P("section", "dp", None),
        P("section", "dp", None),
        P("section", "dp", None),
        P("section", None, "dp", None),
    )
    return jax.shard_map(
        per_device,
        mesh=mesh,
        in_specs=placed,
        out_specs=(
            P("section", "dp", None),
            P("section", "dp", None),
            P("section", "dp", None),
            P("section", None, "dp", None),
        ),
        check_vma=False,
    )
```

time: 436 us -> 324 us (0.74)
  the two profiles are of different devices: /device:TPU:0 before, /device:TPU:1 now
where the time goes in v1:
time: 324 us; the launch traced here: 319 us
  waiting for transfers between devices  159 us (49%)
  Pallas kernels  81.6 us (25%)
  starting transfers between devices  44.6 us (14%)
  other arithmetic  18.5 us (6%)
  local copies, waits for them, and re-layouts  14.3 us (4%)
    ppermute x28, waiting for transfers between devices, shift(): return lax.ppermute(value, AXES, pairs)  159 us
    pallas_call x10, Pallas kernels, whole_call(): pl.pallas_call(kernel, in_specs=[pl.BlockSpec(memory_space=pltpu.SMEM)] +...  68.4 us
    ppermute x28, starting transfers between devices, shift(): return lax.ppermute(value, AXES, pairs)  44.6 us
    unnamed x49, local copies, waits for them, and re-layouts  10.3 us
    convert_element_type x1, other arithmetic, per_device(): rows = new_master[0].astype(jnp.bfloat16)  7.19 us
    pallas_call x1, Pallas kernels, split_halves(): pl.pallas_call(split_kernel, grid_spec=pltpu.PrefetchScalarGridSpec(num_s...  6.65 us
    pallas_call x1, Pallas kernels, merge_halves(): pl.pallas_call(merge_kernel, grid_spec=pltpu.PrefetchScalarGridSpec(num_s...  6.56 us
  transfers between devices with their start and end apart: 28, of which 19 were waited for; matrix products, arithmetic and copies ran while one was open for 3% of the time, Pallas kernels for 15%

profile of v1, /device:TPU:1, one launch (start us, length us, event | category | flops | bytes accessed | tf_op | source)
XLA Modules:
  0.0 319.2 jit_solution(11444646323186530374)
XLA Ops:
  0.6 7.2 %fusion.2 = (bf16[1,1024,512]{2,1,0:T(8,128)(2,1)S(1)}, f32[1,1024,512]{2,1,0:T(8,128)}, f32[1,1024,512]{2,1,0:T(8,128)}, f32[1,1024,512]{2,1,0:T(8,128)}) fusion(f32[1,1024,512]{2,1,0:T(8,128)} %param.5, f32[1,1024,512]{2,1,0:T(8,128)} %param.8, f32[1,1024,512]{2,1,0:T(8,128)} %param.7, f32[1,1024,512]{2,1,0:T(8,128)} %param.6), kind=kLoop, calls=%fused_computation.32 | loop fusion | flops 7340032 | bytes 15728640 | tf_op jit(solution)/shard_map/convert_element_type | solution.py:239
  7.9 1.5 collective-permute-start.1
  9.4 1.5 collective-permute-done.1
  12.5 11.8 %collective-permute-done.2 = bf16[512,512]{1,0:T(8,128)(2,1)S(1)} collective-permute-done((bf16[512,512]{1,0:T(8,128)(2,1)S(1)}, bf16[512,512]{1,0:T(8,128)(2,1)S(1)}, u32[]{:S(2)}, u32[]{:S(2)}) %collective-permute-start.2) | collective-permute-done | bytes 524320 | tf_op jit(solution)/shard_map/ppermute | solution.py:40
  24.5 3.9 %collective-permute-start.3 = (bf16[1024,512]{1,0:T(8,128)(2,1)S(1)}, bf16[1024,512]{1,0:T(8,128)(2,1)S(1)}, u32[]{:S(2)}, u32[]{:S(2)}) collective-permute-start(bf16[1024,512]{1,0:T(8,128)(2,1)S(1)} %pad_maximum_fusion.w0), channel_id=1, source_target_pairs={{0,1},{1,2},{2,3},{3,0},{4,5},{5,6},{6,7},{7,4},{8,11},{9,8},{10,9... | collective-permute-start | bytes 3145736 | tf_op jit(solution)/shard_map/ppermute | solution.py:40
  28.4 6.7 %split_halves.1 = (bf16[256,4096]{1,0:T(8,128)(2,1)}, bf16[256,4096]{1,0:T(8,128)(2,1)}) custom-call(s32[1]{0:T(128)} %bitcast.core_ref, bf16[256,8192]{1,0:T(8,128)(2,1)} %bitcast.8), custom_call_target="tpu_custom_call" | custom-call | bytes 8388608 | tf_op jit(solution)/shard_map/split_halves/pallas_call | solution.py:79
  35.1 5.1 %collective-permute-done.3.w1 = bf16[1024,512]{1,0:T(8,128)(2,1)S(1)} collective-permute-done((bf16[1024,512]{1,0:T(8,128)(2,1)S(1)}, bf16[1024,512]{1,0:T(8,128)(2,1)S(1)}, u32[]{:S(2)}, u32[]{:S(2)}) %collective-permute-start.3) | collective-permute-done | bytes 1048608 | tf_op jit(solution)/shard_map/ppermute | solution.py:40
  40.2 3.1 collective-permute-start.4
  43.3 2.9 collective-permute-start.9
  48.4 12.5 %collective-permute-done.9 = bf16[512,512]{1,0:T(8,128)(2,1)} collective-permute-done((bf16[512,512]{1,0:T(8,128)(2,1)S(1)}, bf16[512,512]{1,0:T(8,128)(2,1)}, u32[]{:S(2)}, u32[]{:S(2)}) %collective-permute-start.9) | collective-permute-done | bytes 524320 | tf_op jit(solution)/shard_map/ppermute | solution.py:40
  62.2 4.3 %broadcast_select_fusion.2 = (bf16[256,4096]{1,0:T(8,128)(2,1)}, bf16[256,4096]{1,0:T(8,128)(2,1)}) fusion(bf16[256,4096]{1,0:T(8,128)(2,1)S(1)} %copy-done.17, bf16[256,4096]{1,0:T(8,128)(2,1)} %collective-permute-done, pred[]{:T(512)S(6)} %eq.4), kind=kLoop, calls=%fused_computation.6 | loop fusion | flops 2097152 | bytes 8388609 | tf_op jit(solution)/shard_map/jit(_where)/select_n | solution.py:233
  66.5 9.6 %collective-permute-done.5.w3 = bf16[1024,512]{1,0:T(8,128)(2,1)S(1)} collective-permute-done((bf16[1024,512]{1,0:T(8,128)(2,1)S(1)}, bf16[1024,512]{1,0:T(8,128)(2,1)S(1)}, u32[]{:S(2)}, u32[]{:S(2)}) %collective-permute-start.5) | collective-permute-done | bytes 1048608 | tf_op jit(solution)/shard_map/ppermute | solution.py:40
  77.1 5.0 %project.5.mine = f32[256,640]{1,0:T(8,128)} custom-call(s32[8]{0:T(128)} %reshape.68.place_ref, bf16[256,4096]{1,0:T(8,128)(2,1)} %get-tuple-element.15.hidden, bf16[1024,512]{1,0:T(8,128)(2,1)} %copy-done.1, bf16[1024,512]{1,0:T(8,128)(2,1)} %copy-done.3, bf16[1024,512]{1,0:T(8,128)(2,1)} %copy-done.4, bf16[1024,512]{1,0:T(8,128)(2,1)} %copy-done.5), custom_call_target="tpu_custom_call" | custom-call | flops 1073741824 | bytes 6946816 | tf_op jit(solution)/shard_map/project/pallas_call | solution.py:168
  82.1 2.8 collective-permute-start.6
  87.8 5.9 %expand.5 = bf16[256,4096]{1,0:T(8,128)(2,1)} custom-call(s32[8]{0:T(128)} %reshape.68.place_ref, bf16[256,4096]{1,0:T(8,128)(2,1)} %get-tuple-element.15.hidden, f32[256,640]{1,0:T(8,128)} %project.5.mine, f32[256,640]{1,0:T(8,128)} %copy-done.22, bf16[1024,512]{1,0:T(8,128)(2,1)} %copy-done.1, bf16[1024,512]{1,0:T(8,128)(2,1)} %copy-done.3, ...), custom_call_target="tpu_custom_call" | custom-call | flops 1073741824 | bytes 9699328 | tf_op jit(solution)/shard_map/expand/pallas_call | solution.py:168
  93.6 2.1 collective-permute-start.7
  95.7 2.9 collective-permute-done.21
  100.6 1.6 collective-permute-start.12
  102.2 10.0 %collective-permute-done.16 = bf16[512,512]{1,0:T(8,128)(2,1)S(1)} collective-permute-done((bf16[512,512]{1,0:T(8,128)(2,1)S(1)}, bf16[512,512]{1,0:T(8,128)(2,1)S(1)}, u32[]{:S(2)}, u32[]{:S(2)}) %collective-permute-start.16) | collective-permute-done | bytes 524320 | tf_op jit(solution)/shard_map/ppermute | solution.py:40
  112.5 2.1 collective-permute-done.12.w2
  114.6 2.8 collective-permute-start.13
  117.3 9.0 %collective-permute-done.17.w1 = bf16[1024,512]{1,0:T(8,128)(2,1)S(1)} collective-permute-done((bf16[1024,512]{1,0:T(8,128)(2,1)S(1)}, bf16[1024,512]{1,0:T(8,128)(2,1)S(1)}, u32[]{:S(2)}, u32[]{:S(2)}) %collective-permute-start.17) | collective-permute-done | bytes 1048608 | tf_op jit(solution)/shard_map/ppermute | solution.py:40
  126.4 2.2 collective-permute-start.18
  128.6 14.7 %collective-permute-done.7 = bf16[256,4096]{1,0:T(8,128)(2,1)S(1)} collective-permute-done((bf16[256,4096]{1,0:T(8,128)(2,1)}, bf16[256,4096]{1,0:T(8,128)(2,1)S(1)}, u32[]{:S(2)}, u32[]{:S(2)}) %collective-permute-start.7) | collective-permute-done | bytes 2097184 | tf_op jit(solution)/shard_map/ppermute | solution.py:40
  143.5 56.0 %collective-permute-done.8 = bf16[256,4096]{1,0:T(8,128)(2,1)S(1)} collective-permute-done((bf16[256,4096]{1,0:T(8,128)(2,1)}, bf16[256,4096]{1,0:T(8,128)(2,1)S(1)}, u32[]{:S(2)}, u32[]{:S(2)}) %collective-permute-start.8) | collective-permute-done | bytes 2097184 | tf_op jit(solution)/shard_map/ppermute | solution.py:40
  199.7 2.0 copy-done
  201.7 7.1 %project.6.mine = f32[512,640]{1,0:T(8,128)} custom-call(s32[8]{0:T(128)} %reshape.68.place_ref, bf16[512,4096]{1,0:T(8,128)(2,1)} %copy-done, bf16[1024,512]{1,0:T(8,128)(2,1)} %copy-done.6, bf16[1024,512]{1,0:T(8,128)(2,1)} %copy-done.9, bf16[1024,512]{1,0:T(8,128)(2,1)} %copy-done.11, bf16[1024,512]{1,0:T(8,128)(2,1)} %collective-permute-done.13.w3), custom_call_target="tpu_custom_call" | custom-call | flops 2147483648 | bytes 9699328 | tf_op jit(solution)/shard_map/project/pallas_call | solution.py:168
  208.7 2.9 collective-permute-start.14
  211.7 1.8 collective-permute-start.22
  214.0 11.7 %collective-permute-done.22.w1 = bf16[1024,512]{1,0:T(8,128)(2,1)S(1)} collective-permute-done((bf16[1024,512]{1,0:T(8,128)(2,1)S(1)}, bf16[1024,512]{1,0:T(8,128)(2,1)S(1)}, u32[]{:S(2)}, u32[]{:S(2)}) %collective-permute-start.22) | collective-permute-done | bytes 1048608 | tf_op jit(solution)/shard_map/ppermute | solution.py:40
  225.8 2.6 collective-permute-start.23
  228.4 8.5 %expand.6.hidden = bf16[512,4096]{1,0:T(8,128)(2,1)} custom-call(s32[8]{0:T(128)} %reshape.68.place_ref, bf16[512,4096]{1,0:T(8,128)(2,1)} %copy-done, f32[512,640]{1,0:T(8,128)} %project.6.mine, f32[512,640]{1,0:T(8,128)} %collective-permute-done.14.theirs, bf16[1024,512]{1,0:T(8,128)(2,1)} %copy-done.6, bf16[1024,512]{1,0:T(8,128)(2,1)} %copy-done.9, ...), custom_call_target="tpu_custom_call" | custom-call | flops 2147483648 | bytes 15204352 | tf_op jit(solution)/shard_map/expand/pallas_call | solution.py:168
  237.9 7.0 %project.7.mine = f32[512,640]{1,0:T(8,128)} custom-call(s32[8]{0:T(128)} %reshape.68.place_ref, bf16[512,4096]{1,0:T(8,128)(2,1)} %expand.6.hidden, bf16[1024,512]{1,0:T(8,128)(2,1)} %copy-done.7, bf16[1024,512]{1,0:T(8,128)(2,1)} %copy-done.10, bf16[1024,512]{1,0:T(8,128)(2,1)} %copy-done.12, bf16[1024,512]{1,0:T(8,128)(2,1)} %copy-done.15), custom_call_target="tpu_custom_call" | custom-call | flops 2147483648 | bytes 9699328 | tf_op jit(solution)/shard_map/project/pallas_call | solution.py:168
  245.0 2.1 collective-permute-start.20
  248.2 2.6 collective-permute-start.24
  251.9 8.6 %expand.7.hidden = bf16[512,4096]{1,0:T(8,128)(2,1)} custom-call(s32[8]{0:T(128)} %reshape.68.place_ref, bf16[512,4096]{1,0:T(8,128)(2,1)} %expand.6.hidden, f32[512,640]{1,0:T(8,128)} %project.7.mine, f32[512,640]{1,0:T(8,128)} %copy-done.20, bf16[1024,512]{1,0:T(8,128)(2,1)} %copy-done.7, bf16[1024,512]{1,0:T(8,128)(2,1)} %copy-done.10, ...), custom_call_target="tpu_custom_call" | custom-call | flops 2147483648 | bytes 15204352 | tf_op jit(solution)/shard_map/expand/pallas_call | solution.py:168
  260.5 2.1 collective-permute-done.24.w3
  263.6 7.0 %project.8.mine = f32[512,640]{1,0:T(8,128)} custom-call(s32[8]{0:T(128)} %reshape.68.place_ref, bf16[512,4096]{1,0:T(8,128)(2,1)} %expand.7.hidden, bf16[1024,512]{1,0:T(8,128)(2,1)} %copy-done.8, bf16[1024,512]{1,0:T(8,128)(2,1)} %copy-done.13, bf16[1024,512]{1,0:T(8,128)(2,1)} %copy-done.14, bf16[1024,512]{1,0:T(8,128)(2,1)} %copy-done.16), custom_call_target="tpu_custom_call" | custom-call | flops 2147483648 | bytes 9699328 | tf_op jit(solution)/shard_map/project/pallas_call | solution.py:168
  270.6 3.7 %collective-permute-start.25 = (f32[512,640]{1,0:T(8,128)}, f32[512,640]{1,0:T(8,128)S(1)}, u32[]{:S(2)}, u32[]{:S(2)}) collective-permute-start(f32[512,640]{1,0:T(8,128)} %project.8.mine), channel_id=1, source_target_pairs={{0,8},{1,9},{2,10},{3,11},{4,12},{5,13},{6,14},{7,15},{8,0},{9,1},... | collective-permute-start | bytes 3932168 | tf_op jit(solution)/shard_map/ppermute | solution.py:40
  274.3 2.9 collective-permute-done.25.theirs
  278.2 8.5 %expand.8 = bf16[512,4096]{1,0:T(8,128)(2,1)} custom-call(s32[8]{0:T(128)} %reshape.68.place_ref, bf16[512,4096]{1,0:T(8,128)(2,1)} %expand.7.hidden, f32[512,640]{1,0:T(8,128)} %project.8.mine, f32[512,640]{1,0:T(8,128)} %copy-done.21, bf16[1024,512]{1,0:T(8,128)(2,1)} %copy-done.8, bf16[1024,512]{1,0:T(8,128)(2,1)} %copy-done.13, ...), custom_call_target="tpu_custom_call" | custom-call | flops 2147483648 | bytes 15204352 | tf_op jit(solution)/shard_map/expand/pallas_call | solution.py:168
  286.8 3.1 slice.18.hidden
  289.9 5.0 %project.9.mine = f32[256,640]{1,0:T(8,128)} custom-call(s32[8]{0:T(128)} %reshape.68.place_ref, bf16[256,4096]{1,0:T(8,128)(2,1)} %slice.18.hidden, bf16[1024,512]{1,0:T(8,128)(2,1)} %copy-done.1, bf16[1024,512]{1,0:T(8,128)(2,1)} %copy-done.3, bf16[1024,512]{1,0:T(8,128)(2,1)} %copy-done.4, bf16[1024,512]{1,0:T(8,128)(2,1)} %copy-done.5), custom_call_target="tpu_custom_call" | custom-call | flops 1073741824 | bytes 6946816 | tf_op jit(solution)/shard_map/project/pallas_call | solution.py:168
  295.3 1.9 collective-permute-done.26.theirs
  298.1 5.9 %expand.9 = bf16[256,4096]{1,0:T(8,128)(2,1)} custom-call(s32[8]{0:T(128)} %reshape.68.place_ref, bf16[256,4096]{1,0:T(8,128)(2,1)} %slice.18.hidden, f32[256,640]{1,0:T(8,128)} %project.9.mine, f32[256,640]{1,0:T(8,128)} %copy-done.23, bf16[1024,512]{1,0:T(8,128)(2,1)} %copy-done.1, bf16[1024,512]{1,0:T(8,128)(2,1)} %copy-done.3, ...), custom_call_target="tpu_custom_call" | custom-call | flops 1073741824 | bytes 9699328 | tf_op jit(solution)/shard_map/expand/pallas_call | solution.py:168
  303.9 3.2 %broadcast_select_fusion = (bf16[256,4096]{1,0:T(8,128)(2,1)S(1)}, bf16[256,4096]{1,0:T(8,128)(2,1)}) fusion(bf16[256,4096]{1,0:T(8,128)(2,1)} %expand.9, pred[]{:T(512)S(6)} %eq.4, bf16[512,4096]{1,0:T(8,128)(2,1)S(1)} %copy-done.2), kind=kLoop, calls=%fused_computation.4 | loop fusion | flops 2097152 | bytes 8388609 | tf_op jit(solution)/shard_map/jit(_where)/select_n | solution.py:261
  307.5 3.8 %collective-permute-done.27.got_ref = bf16[256,4096]{1,0:T(8,128)(2,1)S(1)} collective-permute-done((bf16[256,4096]{1,0:T(8,128)(2,1)S(1)}, bf16[256,4096]{1,0:T(8,128)(2,1)S(1)}, u32[]{:S(2)}, u32[]{:S(2)}) %collective-permute-start.27) | collective-permute-done | bytes 2097184 | tf_op jit(solution)/shard_map/ppermute | solution.py:40
  312.7 6.6 %merge_halves.1 = bf16[256,8192]{1,0:T(8,128)(2,1)} custom-call(s32[1]{0:T(128)} %bitcast.core_ref, bf16[256,4096]{1,0:T(8,128)(2,1)} %get-tuple-element.13.keep_ref, bf16[256,4096]{1,0:T(8,128)(2,1)} %copy-done.18), custom_call_target="tpu_custom_call" | custom-call | bytes 8388608 | tf_op jit(solution)/shard_map/merge_halves/pallas_call | solution.py:103
  (89 shorter events, 20.4 us)
Async XLA Ops:
  7.9 3.0 collective-permute-start.1
  11.1 13.2 %collective-permute-start.2 = (bf16[512,512]{1,0:T(8,128)(2,1)S(1)}, bf16[512,512]{1,0:T(8,128)(2,1)S(1)}, u32[]{:S(2)}, u32[]{:S(2)}) collective-permute-start(bf16[512,512]{1,0:T(8,128)(2,1)S(1)} %get-tuple-element.21), channel_id=1, source_target_pairs={{0,4},{1,5},{2,6},{3,7},{4,0},{5,1},{6,2},{7,3},{8,12},{9,13},{10,... | collective-permute-start | bytes 1572872 | tf_op jit(solution)/shard_map/ppermute | solution.py:40
  24.5 10.6 %copy-start.1 = (bf16[1024,512]{1,0:T(8,128)(2,1)}, bf16[1024,512]{1,0:T(8,128)(2,1)S(1)}, u32[]{:S(2)}) copy-start(bf16[1024,512]{1,0:T(8,128)(2,1)S(1)} %pad_maximum_fusion.w0) | copy-start | bytes 3145732
  24.5 15.7 %collective-permute-start.3 = (bf16[1024,512]{1,0:T(8,128)(2,1)S(1)}, bf16[1024,512]{1,0:T(8,128)(2,1)S(1)}, u32[]{:S(2)}, u32[]{:S(2)}) collective-permute-start(bf16[1024,512]{1,0:T(8,128)(2,1)S(1)} %pad_maximum_fusion.w0), channel_id=1, source_target_pairs={{0,1},{1,2},{2,3},{3,0},{4,5},{5,6},{6,7},{7,4},{8,11},{9,8},{10,9... | collective-permute-start | bytes 3145736 | tf_op jit(solution)/shard_map/ppermute | solution.py:40
  35.1 27.1 %collective-permute-start = (bf16[256,4096]{1,0:T(8,128)(2,1)}, bf16[256,4096]{1,0:T(8,128)(2,1)}, u32[]{:S(2)}, u32[]{:S(2)}) collective-permute-start(bf16[256,4096]{1,0:T(8,128)(2,1)} %get-tuple-element.6), channel_id=1, source_target_pairs={{0,8},{1,9},{2,10},{3,11},{4,12},{5,13},{6,14},{7,15},{8,0},{9,1},... | collective-permute-start | bytes 6291464 | tf_op jit(solution)/shard_map/ppermute | solution.py:40
  40.2 26.3 %copy-start.3 = (bf16[1024,512]{1,0:T(8,128)(2,1)}, bf16[1024,512]{1,0:T(8,128)(2,1)S(1)}, u32[]{:S(2)}) copy-start(bf16[1024,512]{1,0:T(8,128)(2,1)S(1)} %collective-permute-done.3.w1) | copy-start | bytes 3145732
  40.2 22.0 %collective-permute-start.4 = (bf16[1024,512]{1,0:T(8,128)(2,1)S(1)}, bf16[1024,512]{1,0:T(8,128)(2,1)S(1)}, u32[]{:S(2)}, u32[]{:S(2)}) collective-permute-start(bf16[1024,512]{1,0:T(8,128)(2,1)S(1)} %collective-permute-done.3.w1), channel_id=1, source_target_pairs={{0,1},{1,2},{2,3},{3,0},{4,5},{5,6},{6,7},{7,4},{8,11},{9,8},{10,9... | collective-permute-start | bytes 3145736 | tf_op jit(solution)/shard_map/ppermute | solution.py:40
  43.3 17.7 %collective-permute-start.9 = (bf16[512,512]{1,0:T(8,128)(2,1)S(1)}, bf16[512,512]{1,0:T(8,128)(2,1)}, u32[]{:S(2)}, u32[]{:S(2)}) collective-permute-start(bf16[512,512]{1,0:T(8,128)(2,1)S(1)} %get-tuple-element.20), channel_id=1, source_target_pairs={{0,32},{1,33},{2,34},{3,35},{4,36},{5,37},{6,38},{7,39},{8,40},{9,... | collective-permute-start | bytes 1572872 | tf_op jit(solution)/shard_map/ppermute | solution.py:40
  46.9 15.3 %copy-start.17 = (bf16[256,4096]{1,0:T(8,128)(2,1)S(1)}, bf16[256,4096]{1,0:T(8,128)(2,1)}, u32[]{:S(2)}) copy-start(bf16[256,4096]{1,0:T(8,128)(2,1)} %get-tuple-element.7) | copy-start | bytes 6291460
  48.0 36.9 %collective-permute-start.15 = (bf16[1024,512]{1,0:T(8,128)(2,1)}, bf16[1024,512]{1,0:T(8,128)(2,1)S(1)}, u32[]{:S(2)}, u32[]{:S(2)}) collective-permute-start(bf16[1024,512]{1,0:T(8,128)(2,1)} %pad_maximum_fusion.2), channel_id=1, source_target_pairs={{0,16},{1,17},{2,18},{3,19},{4,20},{5,21},{6,22},{7,23},{8,24},{9,... | collective-permute-start | bytes 3145736 | tf_op jit(solution)/shard_map/ppermute | solution.py:40
  61.0 24.4 %collective-permute-start.10 = (bf16[512,512]{1,0:T(8,128)(2,1)}, bf16[512,512]{1,0:T(8,128)(2,1)S(1)}, u32[]{:S(2)}, u32[]{:S(2)}) collective-permute-start(bf16[512,512]{1,0:T(8,128)(2,1)} %collective-permute-done.9), channel_id=1, source_target_pairs={{0,4},{1,5},{2,6},{3,7},{4,0},{5,1},{6,2},{7,3},{8,12},{9,13},{10,... | collective-permute-start | bytes 1572872 | tf_op jit(solution)/shard_map/ppermute | solution.py:40
  62.2 4.3 %copy-start.4 = (bf16[1024,512]{1,0:T(8,128)(2,1)}, bf16[1024,512]{1,0:T(8,128)(2,1)S(1)}, u32[]{:S(2)}) copy-start(bf16[1024,512]{1,0:T(8,128)(2,1)S(1)} %collective-permute-done.4.w2) | copy-start | bytes 3145732
  62.2 13.9 %collective-permute-start.5 = (bf16[1024,512]{1,0:T(8,128)(2,1)S(1)}, bf16[1024,512]{1,0:T(8,128)(2,1)S(1)}, u32[]{:S(2)}, u32[]{:S(2)}) collective-permute-start(bf16[1024,512]{1,0:T(8,128)(2,1)S(1)} %collective-permute-done.4.w2), channel_id=1, source_target_pairs={{0,1},{1,2},{2,3},{3,0},{4,5},{5,6},{6,7},{7,4},{8,11},{9,8},{10,9... | collective-permute-start | bytes 3145736 | tf_op jit(solution)/shard_map/ppermute | solution.py:40
  82.1 4.8 %collective-permute-start.6 = (f32[256,640]{1,0:T(8,128)}, f32[256,640]{1,0:T(8,128)S(1)}, u32[]{:S(2)}, u32[]{:S(2)}) collective-permute-start(f32[256,640]{1,0:T(8,128)} %project.5.mine), channel_id=1, source_target_pairs={{0,8},{1,9},{2,10},{3,11},{4,12},{5,13},{6,14},{7,15},{8,0},{9,1},... | collective-permute-start | bytes 1966088 | tf_op jit(solution)/shard_map/ppermute | solution.py:40
  85.0 13.6 %collective-permute-start.21 = (bf16[512,512]{1,0:T(8,128)(2,1)S(1)}, bf16[512,512]{1,0:T(8,128)(2,1)S(1)}, u32[]{:S(2)}, u32[]{:S(2)}) collective-permute-start(bf16[512,512]{1,0:T(8,128)(2,1)S(1)} %slice.17), channel_id=1, source_target_pairs={{0,4},{1,5},{2,6},{3,7},{4,0},{5,1},{6,2},{7,3},{8,12},{9,13},{10,... | collective-permute-start | bytes 1572872 | tf_op jit(solution)/shard_map/ppermute | solution.py:40
  86.6 7.1 %copy-start.6 = (bf16[1024,512]{1,0:T(8,128)(2,1)}, bf16[1024,512]{1,0:T(8,128)(2,1)S(1)}, u32[]{:S(2)}) copy-start(bf16[1024,512]{1,0:T(8,128)(2,1)S(1)} %pad_maximum_fusion.1.w0) | copy-start | bytes 3145732
  86.6 14.0 %collective-permute-start.11 = (bf16[1024,512]{1,0:T(8,128)(2,1)S(1)}, bf16[1024,512]{1,0:T(8,128)(2,1)S(1)}, u32[]{:S(2)}, u32[]{:S(2)}) collective-permute-start(bf16[1024,512]{1,0:T(8,128)(2,1)S(1)} %pad_maximum_fusion.1.w0), channel_id=1, source_target_pairs={{0,1},{1,2},{2,3},{3,0},{4,5},{5,6},{6,7},{7,4},{8,11},{9,8},{10,9... | collective-permute-start | bytes 3145736 | tf_op jit(solution)/shard_map/ppermute | solution.py:40
  93.6 49.7 %collective-permute-start.7 = (bf16[256,4096]{1,0:T(8,128)(2,1)}, bf16[256,4096]{1,0:T(8,128)(2,1)S(1)}, u32[]{:S(2)}, u32[]{:S(2)}) collective-permute-start(bf16[256,4096]{1,0:T(8,128)(2,1)} %expand.5), channel_id=1, source_target_pairs={{0,32},{1,33},{2,34},{3,35},{4,36},{5,37},{6,38},{7,39},{8,40},{9,... | collective-permute-start | bytes 6291464 | tf_op jit(solution)/shard_map/ppermute | solution.py:40
  99.5 12.7 %collective-permute-start.16 = (bf16[512,512]{1,0:T(8,128)(2,1)S(1)}, bf16[512,512]{1,0:T(8,128)(2,1)S(1)}, u32[]{:S(2)}, u32[]{:S(2)}) collective-permute-start(bf16[512,512]{1,0:T(8,128)(2,1)S(1)} %get-tuple-element.22), channel_id=1, source_target_pairs={{0,4},{1,5},{2,6},{3,7},{4,0},{5,1},{6,2},{7,3},{8,12},{9,13},{10,... | collective-permute-start | bytes 1572872 | tf_op jit(solution)/shard_map/ppermute | solution.py:40
  99.5 100.0 %collective-permute-start.8 = (bf16[256,4096]{1,0:T(8,128)(2,1)}, bf16[256,4096]{1,0:T(8,128)(2,1)S(1)}, u32[]{:S(2)}, u32[]{:S(2)}) collective-permute-start(bf16[256,4096]{1,0:T(8,128)(2,1)} %get-tuple-element.14), channel_id=1, source_target_pairs={{0,32},{1,33},{2,34},{3,35},{4,36},{5,37},{6,38},{7,39},{8,40},{9,... | collective-permute-start | bytes 6291464 | tf_op jit(solution)/shard_map/ppermute | solution.py:40
  100.6 11.7 %copy-start.9 = (bf16[1024,512]{1,0:T(8,128)(2,1)}, bf16[1024,512]{1,0:T(8,128)(2,1)S(1)}, u32[]{:S(2)}) copy-start(bf16[1024,512]{1,0:T(8,128)(2,1)S(1)} %collective-permute-done.11.w1) | copy-start | bytes 3145732
  100.6 13.9 %collective-permute-start.12 = (bf16[1024,512]{1,0:T(8,128)(2,1)S(1)}, bf16[1024,512]{1,0:T(8,128)(2,1)S(1)}, u32[]{:S(2)}, u32[]{:S(2)}) collective-permute-start(bf16[1024,512]{1,0:T(8,128)(2,1)S(1)} %collective-permute-done.11.w1), channel_id=1, source_target_pairs={{0,1},{1,2},{2,3},{3,0},{4,5},{5,6},{6,7},{7,4},{8,11},{9,8},{10,9... | collective-permute-start | bytes 3145736 | tf_op jit(solution)/shard_map/ppermute | solution.py:40
  112.4 31.1 %copy-start.7 = (bf16[1024,512]{1,0:T(8,128)(2,1)}, bf16[1024,512]{1,0:T(8,128)(2,1)S(1)}, u32[]{:S(2)}) copy-start(bf16[1024,512]{1,0:T(8,128)(2,1)S(1)} %pad_maximum_fusion.3.w0) | copy-start | bytes 3145732
  112.4 14.0 %collective-permute-start.17 = (bf16[1024,512]{1,0:T(8,128)(2,1)S(1)}, bf16[1024,512]{1,0:T(8,128)(2,1)S(1)}, u32[]{:S(2)}, u32[]{:S(2)}) collective-permute-start(bf16[1024,512]{1,0:T(8,128)(2,1)S(1)} %pad_maximum_fusion.3.w0), channel_id=1, source_target_pairs={{0,1},{1,2},{2,3},{3,0},{4,5},{5,6},{6,7},{7,4},{8,11},{9,8},{10,9... | collective-permute-start | bytes 3145736 | tf_op jit(solution)/shard_map/ppermute | solution.py:40
  114.6 28.9 %copy-start.11 = (bf16[1024,512]{1,0:T(8,128)(2,1)}, bf16[1024,512]{1,0:T(8,128)(2,1)S(1)}, u32[]{:S(2)}) copy-start(bf16[1024,512]{1,0:T(8,128)(2,1)S(1)} %collective-permute-done.12.w2) | copy-start | bytes 3145732
  114.6 85.1 %collective-permute-start.13 = (bf16[1024,512]{1,0:T(8,128)(2,1)S(1)}, bf16[1024,512]{1,0:T(8,128)(2,1)}, u32[]{:S(2)}, u32[]{:S(2)}) collective-permute-start(bf16[1024,512]{1,0:T(8,128)(2,1)S(1)} %collective-permute-done.12.w2), channel_id=1, source_target_pairs={{0,1},{1,2},{2,3},{3,0},{4,5},{5,6},{6,7},{7,4},{8,11},{9,8},{10,9... | collective-permute-start | bytes 3145736 | tf_op jit(solution)/shard_map/ppermute | solution.py:40
  126.4 17.1 %copy-start.10 = (bf16[1024,512]{1,0:T(8,128)(2,1)}, bf16[1024,512]{1,0:T(8,128)(2,1)S(1)}, u32[]{:S(2)}) copy-start(bf16[1024,512]{1,0:T(8,128)(2,1)S(1)} %collective-permute-done.17.w1) | copy-start | bytes 3145732
  126.4 87.1 %collective-permute-start.18 = (bf16[1024,512]{1,0:T(8,128)(2,1)S(1)}, bf16[1024,512]{1,0:T(8,128)(2,1)S(1)}, u32[]{:S(2)}, u32[]{:S(2)}) collective-permute-start(bf16[1024,512]{1,0:T(8,128)(2,1)S(1)} %collective-permute-done.17.w1), channel_id=1, source_target_pairs={{0,1},{1,2},{2,3},{3,0},{4,5},{5,6},{6,7},{7,4},{8,11},{9,8},{10,9... | collective-permute-start | bytes 3145736 | tf_op jit(solution)/shard_map/ppermute | solution.py:40
  199.6 2.0 copy-start
  201.7 10.0 %copy-start.19 = (bf16[512,512]{1,0:T(8,128)(2,1)S(1)}, bf16[512,512]{1,0:T(8,128)(2,1)}, u32[]{:S(2)}) copy-start(bf16[512,512]{1,0:T(8,128)(2,1)} %get-tuple-element.17) | copy-start | bytes 1572868
  208.7 19.7 %collective-permute-start.14 = (f32[512,640]{1,0:T(8,128)}, f32[512,640]{1,0:T(8,128)}, u32[]{:S(2)}, u32[]{:S(2)}) collective-permute-start(f32[512,640]{1,0:T(8,128)} %project.6.mine), channel_id=1, source_target_pairs={{0,8},{1,9},{2,10},{3,11},{4,12},{5,13},{6,14},{7,15},{8,0},{9,1},... | collective-permute-start | bytes 3932168 | tf_op jit(solution)/shard_map/ppermute | solution.py:40
  211.7 25.2 %copy-start.8 = (bf16[1024,512]{1,0:T(8,128)(2,1)}, bf16[1024,512]{1,0:T(8,128)(2,1)S(1)}, u32[]{:S(2)}) copy-start(bf16[1024,512]{1,0:T(8,128)(2,1)S(1)} %pad_maximum_fusion.4.w0) | copy-start | bytes 3145732
  211.7 14.0 %collective-permute-start.22 = (bf16[1024,512]{1,0:T(8,128)(2,1)S(1)}, bf16[1024,512]{1,0:T(8,128)(2,1)S(1)}, u32[]{:S(2)}, u32[]{:S(2)}) collective-permute-start(bf16[1024,512]{1,0:T(8,128)(2,1)S(1)} %pad_maximum_fusion.4.w0), channel_id=1, source_target_pairs={{0,1},{1,2},{2,3},{3,0},{4,5},{5,6},{6,7},{7,4},{8,11},{9,8},{10,9... | collective-permute-start | bytes 3145736 | tf_op jit(solution)/shard_map/ppermute | solution.py:40
  213.5 23.4 %copy-start.12 = (bf16[1024,512]{1,0:T(8,128)(2,1)}, bf16[1024,512]{1,0:T(8,128)(2,1)S(1)}, u32[]{:S(2)}) copy-start(bf16[1024,512]{1,0:T(8,128)(2,1)S(1)} %collective-permute-done.18.w2) | copy-start | bytes 3145732
  213.5 23.5 %collective-permute-start.19 = (bf16[1024,512]{1,0:T(8,128)(2,1)S(1)}, bf16[1024,512]{1,0:T(8,128)(2,1)S(1)}, u32[]{:S(2)}, u32[]{:S(2)}) collective-permute-start(bf16[1024,512]{1,0:T(8,128)(2,1)S(1)} %collective-permute-done.18.w2), channel_id=1, source_target_pairs={{0,1},{1,2},{2,3},{3,0},{4,5},{5,6},{6,7},{7,4},{8,11},{9,8},{10,9... | collective-permute-start | bytes 3145736 | tf_op jit(solution)/shard_map/ppermute | solution.py:40
  225.8 11.2 %copy-start.13 = (bf16[1024,512]{1,0:T(8,128)(2,1)}, bf16[1024,512]{1,0:T(8,128)(2,1)S(1)}, u32[]{:S(2)}) copy-start(bf16[1024,512]{1,0:T(8,128)(2,1)S(1)} %collective-permute-done.22.w1) | copy-start | bytes 3145732
  225.8 22.5 %collective-permute-start.23 = (bf16[1024,512]{1,0:T(8,128)(2,1)S(1)}, bf16[1024,512]{1,0:T(8,128)(2,1)S(1)}, u32[]{:S(2)}, u32[]{:S(2)}) collective-permute-start(bf16[1024,512]{1,0:T(8,128)(2,1)S(1)} %collective-permute-done.22.w1), channel_id=1, source_target_pairs={{0,1},{1,2},{2,3},{3,0},{4,5},{5,6},{6,7},{7,4},{8,11},{9,8},{10,9... | collective-permute-start | bytes 3145736 | tf_op jit(solution)/shard_map/ppermute | solution.py:40
  245.0 5.9 %collective-permute-start.20 = (f32[512,640]{1,0:T(8,128)}, f32[512,640]{1,0:T(8,128)S(1)}, u32[]{:S(2)}, u32[]{:S(2)}) collective-permute-start(f32[512,640]{1,0:T(8,128)} %project.7.mine), channel_id=1, source_target_pairs={{0,8},{1,9},{2,10},{3,11},{4,12},{5,13},{6,14},{7,15},{8,0},{9,1},... | collective-permute-start | bytes 3932168 | tf_op jit(solution)/shard_map/ppermute | solution.py:40
  248.2 12.3 %copy-start.14 = (bf16[1024,512]{1,0:T(8,128)(2,1)}, bf16[1024,512]{1,0:T(8,128)(2,1)S(1)}, u32[]{:S(2)}) copy-start(bf16[1024,512]{1,0:T(8,128)(2,1)S(1)} %collective-permute-done.23.w2) | copy-start | bytes 3145732
  248.2 14.4 %collective-permute-start.24 = (bf16[1024,512]{1,0:T(8,128)(2,1)S(1)}, bf16[1024,512]{1,0:T(8,128)(2,1)S(1)}, u32[]{:S(2)}, u32[]{:S(2)}) collective-permute-start(bf16[1024,512]{1,0:T(8,128)(2,1)S(1)} %collective-permute-done.23.w2), channel_id=1, source_target_pairs={{0,1},{1,2},{2,3},{3,0},{4,5},{5,6},{6,7},{7,4},{8,11},{9,8},{10,9... | collective-permute-start | bytes 3145736 | tf_op jit(solution)/shard_map/ppermute | solution.py:40
  250.8 1.1 copy-start.20
  262.6 1.0 copy-start.16
  270.6 6.6 %collective-permute-start.25 = (f32[512,640]{1,0:T(8,128)}, f32[512,640]{1,0:T(8,128)S(1)}, u32[]{:S(2)}, u32[]{:S(2)}) collective-permute-start(f32[512,640]{1,0:T(8,128)} %project.8.mine), channel_id=1, source_target_pairs={{0,8},{1,9},{2,10},{3,11},{4,12},{5,13},{6,14},{7,15},{8,0},{9,1},... | collective-permute-start | bytes 3932168 | tf_op jit(solution)/shard_map/ppermute | solution.py:40
  277.2 1.1 copy-start.21
  294.9 9.0 %copy-start.2 = (bf16[512,4096]{1,0:T(8,128)(2,1)S(1)}, bf16[512,4096]{1,0:T(8,128)(2,1)}, u32[]{:S(2)}) copy-start(bf16[512,4096]{1,0:T(8,128)(2,1)} %expand.8) | copy-start | bytes 12582916
  294.9 2.3 collective-permute-start.26
  307.1 4.2 %collective-permute-start.27 = (bf16[256,4096]{1,0:T(8,128)(2,1)S(1)}, bf16[256,4096]{1,0:T(8,128)(2,1)S(1)}, u32[]{:S(2)}, u32[]{:S(2)}) collective-permute-start(bf16[256,4096]{1,0:T(8,128)(2,1)S(1)} %get-tuple-element.12), channel_id=1, source_target_pairs={{0,8},{1,9},{2,10},{3,11},{4,12},{5,13},{6,14},{7,15},{8,0},{9,1},... | collective-permute-start | bytes 6291464 | tf_op jit(solution)/shard_map/ppermute | solution.py:40
  311.3 1.4 copy-start.18
  (4 other events, 3.6 us)
